TPU v7x, 32 devices: a whole 2x2x4 slice. The times are simulated.
32 devices in a mesh: grp: 2 (over y), aa: 4 (over x, core), ba: 4 (over z).
Axes of the slice: x: 2, y: 2, z: 4, core: 2. Of those that a mesh axis runs over, the one named last changes fastest.
Arguments:
- gate_first: bfloat16 [2048, 8192], P(('grp', 'ba'), 'aa'), parts along dimension 0, may hold values from -6 to 6
- up_first: bfloat16 [2048, 8192], P(('grp', 'ba'), 'aa'), parts along dimension 0, may hold values from -6 to 6
- down_first: bfloat16 [8192, 2048], P('aa', ('grp', 'ba')), parts along dimension 1, may hold values from -6 to 6
- gate_second: bfloat16 [57344, 8192], P(('grp', 'ba'), 'aa'), parts along dimension 0, may hold values from -0.0625 to 0.0625
- up_second: bfloat16 [57344, 8192], P(('grp', 'ba'), 'aa'), parts along dimension 0, may hold values from -0.0625 to 0.0625
- down_second: bfloat16 [8192, 57344], P('aa', ('grp', 'ba')), parts along dimension 1, may hold values from -0.0625 to 0.0625
- perm: int32 [16384], P('grp'), parts along dimension 0, may hold values from 0 to 8191, each once
Outputs:
- cost: float32 [2048, 28672], P(('grp', 'aa'), 'ba'), parts along dimension 0
There are 2 independent parts, one for each index of `grp`. A program takes and returns all parts, laid end to end along the dimension named above; each array names one. Nothing has to cross between parts.
All inputs are finite; a program needn't handle non-finite values.
Results may differ from a plain program's by a relative error of at most 0.0003.
Values may be sent and summed in bfloat16 or wider, within the bound.
A program may use at most 320 MiB of HBM per device.

v0:
```python
import jax
import jax.numpy as jnp
from jax import lax
from jax.sharding import PartitionSpec as P


def partial_cost(panel_rows, gate_second, up_second, down_second):
    contract = (((1,), (1,)), ((), ()))
    summed = lax.dot_general(
        panel_rows[0], gate_second, contract, preferred_element_type=jnp.float32
    )
    summed = summed + lax.dot_general(
        panel_rows[1], up_second, contract, preferred_element_type=jnp.float32
    )
    return summed + jnp.dot(panel_rows[2], down_second, preferred_element_type=jnp.float32)


def shards(gate_first, up_first, down_first, gate_second, up_second, down_second, perm):
    stacked = jnp.stack([gate_first, up_first, jnp.transpose(down_first)])
    features = lax.all_gather(stacked, "aa", axis=2, tiled=True)
    columns_dev = gate_second.shape[1]
    offset = lax.axis_index("aa") * columns_dev
    count_d = perm.shape[0]
    inverse = jnp.zeros((count_d,), jnp.int32).at[perm].set(jnp.arange(count_d, dtype=jnp.int32))
    chosen = lax.dynamic_slice_in_dim(inverse, offset, columns_dev)
    reordered = jnp.take(features, chosen, axis=2)
    gathered = lax.all_gather(reordered, "ba", axis=1, tiled=True)
    return lax.psum_scatter(
        partial_cost(gathered, gate_second, up_second, down_second),
        "aa",
        scatter_dimension=0,
        tiled=True,
    )


def solution(mesh):
    placed = (
        P(("grp", "ba"), "aa"),
        P(("grp", "ba"), "aa"),
        P("aa", ("grp", "ba")),
        P(("grp", "ba"), "aa"),
        P(("grp", "ba"), "aa"),
        P("aa", ("grp", "ba")),
        P("grp"),
    )
    return jax.shard_map(
        shards, mesh=mesh, in_specs=placed, out_specs=P(("grp", "aa"), "ba"), check_vma=False
    )
```

profile of v0, /device:TPU:1, one launch (start us, length us, event | category | flops | bytes accessed | tf_op | source)
XLA Modules:
  0.0 867.9 jit_solution(2057364734275471165)
XLA Ops:
  6.5 0.0 copy-start.2
  6.5 0.0 all-gather.3.cloned.1.call-start
  6.5 1.5 copy.19
  8.0 3.5 pad_maximum_fusion
  11.6 0.0 all-gather.3.cloned.1.call-update
  11.6 0.0 all-gather.5.cloned.1.call-start
  11.7 0.0 copy-done.2
  11.7 30.5 %scatter_custom_fusion = s32[8192]{0:T(1024)S(1)} fusion(s32[8192]{0:T(1024)S(1)} %compare_select_fusion, s32[8192]{0:T(1024)S(1)} %iota.3, s32[]{:T(128)} %constant.8.clone.1), kind=kCustom, calls=%fused_computation.12 | custom fusion | bytes 32772 | tf_op jit(solution)/shard_map/scatter | solution.py:24
  42.2 54.1 %all-gather.3.cloned.1.call-done = bf16[3,256,8192]{2,1,0:T(8,128)(2,1)} async-done(((bf16[3,256,2048]{2,1,0:T(8,128)(2,1)}), bf16[3,256,8192]{2,1,0:T(8,128)(2,1)}) %all-gather.3.cloned.1.call-update) | async-done | bytes 12582928 | tf_op jit(solution)/shard_map/all_gather | solution.py:20
  96.4 24.9 %copy.20 = bf16[3,256,8192]{1,0,2:T(4,128)(2,1)} copy(bf16[3,256,8192]{2,1,0:T(8,128)(2,1)} %all-gather.3.cloned.1.call-done) | data formatting | bytes 25165824 | tf_op jit(solution)/shard_map/all_gather | solution.py:20
  121.3 22.3 %gather_fusion = bf16[2048,3,256]{2,1,0:T(4,128)(2,1)} fusion(bf16[3,256,8192]{1,0,2:T(4,128)(2,1)} %copy.20, s32[2048]{0:T(1024)S(1)} %fusion.7), kind=kCustom, calls=%fused_computation | custom fusion | bytes 6299648 | tf_op jit(solution)/shard_map/jit(_take)/gather | solution.py:26
  143.6 10.9 %select_bitcast_fusion = bf16[3,256,2048]{1,0,2:T(4,128)(2,1)} fusion(bf16[2048,3,256]{2,1,0:T(4,128)(2,1)} %gather_fusion, pred[2048]{0:T(1024)(128)(4,1)S(1)} %compare_and_fusion), kind=kLoop, calls=%fused_computation.8 | loop fusion | flops 1572864 | bytes 6293504 | tf_op jit(solution)/shard_map/jit(_take)/select_n | solution.py:26
  154.6 0.0 all-gather.5.cloned.1.call-update
  154.6 0.2 reduce-scatter.2.cloned.1.call-start
  154.8 285.9 %all-gather.5.cloned.1.call-done = bf16[3,1024,2048]{1,0,2:T(4,128)(2,1)} async-done(((bf16[3,256,2048]{1,0,2:T(4,128)(2,1)}), bf16[3,1024,2048]{1,0,2:T(4,128)(2,1)}) %all-gather.5.cloned.1.call-update) | async-done | bytes 12582928 | tf_op jit(solution)/shard_map/all_gather | solution.py:27
  440.7 30.1 %fusion.8 = (bf16[1,1024,2048]{1,0,2:T(2,128)(2,1)}, bf16[1,1024,2048]{1,0,2:T(2,128)(2,1)}, bf16[1,1024,2048]{1,0,2:T(2,128)(2,1)}) fusion(bf16[3,1024,2048]{1,0,2:T(4,128)(2,1)} %all-gather.5.cloned.1.call-done), kind=kLoop, calls=%fused_computation.16 | loop fusion | bytes 25165824 | tf_op jit(solution)/shard_map/slice | solution.py:13
  470.8 20.1 %copy.22 = bf16[1,1024,2048]{2,1,0:T(8,128)(2,1)} copy(bf16[1,1024,2048]{1,0,2:T(2,128)(2,1)} %get-tuple-element.5) | data formatting | bytes 8388608 | tf_op jit(solution)/shard_map/slice | solution.py:13
  490.9 19.8 %copy.23 = bf16[1,1024,2048]{2,1,0:T(8,128)(2,1)} copy(bf16[1,1024,2048]{1,0,2:T(2,128)(2,1)} %get-tuple-element.6) | data formatting | bytes 8388608 | tf_op jit(solution)/shard_map/slice | solution.py:15
  510.8 20.0 %copy.21 = bf16[1,1024,2048]{2,1,0:T(8,128)(2,1)} copy(bf16[1,1024,2048]{1,0,2:T(2,128)(2,1)} %get-tuple-element.7) | data formatting | bytes 8388608 | tf_op jit(solution)/shard_map/slice | solution.py:10
  530.8 0.0 copy-start.1
  530.8 37.5 %fusion.3 = f32[1024,7168]{1,0:T(8,128)} fusion(bf16[7168,2048]{1,0:T(8,128)(2,1)} %param.10, bf16[1,1024,2048]{2,1,0:T(8,128)(2,1)} %copy.21), kind=kOutput, calls=%fused_computation.6 | convolution fusion | flops 30064771072 | bytes 62914560 | tf_op jit(solution)/shard_map/dot_general | solution.py:9
  568.3 0.0 copy-done.1
  568.3 0.0 copy-start
  568.3 36.0 %fusion = f32[1024,7168]{1,0:T(8,128)} fusion(bf16[2048,7168]{1,0:T(8,128)(2,1)} %param.12, bf16[1,1024,2048]{2,1,0:T(8,128)(2,1)S(1)} %copy-done.1), kind=kOutput, calls=%fused_computation.3 | convolution fusion | flops 30064771072 | bytes 62914560 | tf_op jit(solution)/shard_map/dot_general | solution.py:15
  604.3 0.0 copy-done
  604.3 51.0 %add_add_fusion = f32[1024,7168]{1,0:T(8,128)} fusion(f32[1024,7168]{1,0:T(8,128)} %fusion, f32[1024,7168]{1,0:T(8,128)} %fusion.3, bf16[7168,2048]{1,0:T(8,128)(2,1)} %param.11, bf16[1,1024,2048]{2,1,0:T(8,128)(2,1)S(1)} %copy-done), kind=kOutput, calls=%fused_computation.2 | convolution fusion | flops 30079451136 | bytes 121634816 | tf_op jit(solution)/shard_map/dot_general | solution.py:12
  655.3 0.0 reduce-scatter.2.cloned.1.call-update
  655.3 206.1 %reduce-scatter.2.cloned.1.call-done = f32[256,7168]{1,0:T(8,128)} async-done(((f32[1024,7168]{1,0:T(8,128)}), f32[256,7168]{1,0:T(8,128)}) %reduce-scatter.2.cloned.1.call-update) | async-done | bytes 7340048 | tf_op jit(solution)/shard_map/reduce_scatter | solution.py:28
  (4 shorter events, 0.0 us)
Async XLA Ops:
  6.5 5.1 copy-start.2
  6.5 89.8 %all-gather.3.cloned.1.call-start = ((), (), s32[]{:S(2)}) async-start(), calls=%async_computation.1 | async-start | bytes 15728640 | tf_op jit(solution)/shard_map/all_gather | solution.py:20
  11.6 429.1 %all-gather.5.cloned.1.call-start = ((), (), s32[]{:S(2)}) async-start(), calls=%async_computation.2 | async-start | bytes 20971520 | tf_op jit(solution)/shard_map/all_gather | solution.py:27
  154.6 706.8 %reduce-scatter.2.cloned.1.call-start = ((), (), s32[]{:S(2)}) async-start(), calls=%async_computation.3 | async-start | bytes 36700160 | tf_op jit(solution)/shard_map/reduce_scatter | solution.py:28
  530.8 37.5 %copy-start.1 = (bf16[1,1024,2048]{2,1,0:T(8,128)(2,1)S(1)}, bf16[1,1024,2048]{2,1,0:T(8,128)(2,1)}, u32[]{:S(2)}) copy-start(bf16[1,1024,2048]{2,1,0:T(8,128)(2,1)} %copy.23) | copy-start | bytes 12582916
  568.3 36.0 %copy-start = (bf16[1,1024,2048]{2,1,0:T(8,128)(2,1)S(1)}, bf16[1,1024,2048]{2,1,0:T(8,128)(2,1)}, u32[]{:S(2)}) copy-start(bf16[1,1024,2048]{2,1,0:T(8,128)(2,1)} %copy.22) | copy-start | bytes 12582916
Sparse Core Ops, SparseCore 0:
  11.7 84.5 all-gather.2
  154.7 285.9 all-gather.4
  655.4 205.9 reduce-scatter.1
where the time goes:
time: 871 us; the launch traced here: 868 us
  waiting for transfers between devices  546 us (63%)
  local copies, waits for them, and re-layouts  169 us (19%)
  matrix products  124 us (14%)
  other arithmetic  14.5 us (2%)
  between operations  13.2 us (2%)
    all_gather x1, waiting for transfers between devices, shards(): gathered = lax.all_gather(reordered, 'ba', axis=1, tiled=True)  286 us
    reduce_scatter x1, waiting for transfers between devices, shards(): lax.psum_scatter(partial_cost(gathered, gate_second, up_second, down_seco...  206 us
    all_gather x1, waiting for transfers between devices, shards(): features = lax.all_gather(stacked, 'aa', axis=2, tiled=True)  54.1 us
    dot_general x1, matrix products, partial_cost(): lax.dot_general(panel_rows[1], up_second, contract, preferred_element_typ...  51 us
    slice x2, local copies, waits for them, and re-layouts, partial_cost(): panel_rows[1]  50.2 us
    dot_general x1, matrix products, partial_cost(): lax.dot_general(panel_rows[0], gate_second, contract, preferred_element_t...  37.5 us
    dot_general x1, matrix products, partial_cost(): jnp.dot(panel_rows[2], down_second, preferred_element_type=jnp.float32)  36 us
    scatter x1, local copies, waits for them, and re-layouts, shards(): jnp.zeros((count_d,), jnp.int32).at[perm]  30.5 us
  transfers between devices with their start and end apart: 3, of which 3 were waited for; matrix products, arithmetic and copies ran while one was open for 4% of the time, Pallas kernels for 0%

commit v1 on v0

v1 whole, which is shorter than its diff:
```python
import functools

import jax
import jax.numpy as jnp
from jax import lax
from jax.experimental import pallas as pl
from jax.experimental.pallas import tpu as pltpu
from jax.sharding import PartitionSpec as P

MESH = pl.DeviceIdType.MESH
NT_DIMS = (((1,), (1,)), ((), ()))


def kernel(
    stages, blocks, rows, tile, e_tile,
    first_ref, perm_ref, gate_ref, up_ref, down_ref,
    own_ref, far_ref,
    raw, panel, part, near, w_gate, w_up, w_down, onehot,
    w_sem, raw_here, raw_recv, raw_send, z_recv, z_send, near_recv, near_send, far_recv, far_send, own_sem, credit,
):
    columns = first_ref.shape[2]
    units = gate_ref.shape[0]
    half = units // 2
    group = blocks // 4
    a = lax.axis_index("aa")
    b = lax.axis_index("ba")
    core = a + 1 - 2 * (a % 2)
    chip = (a + 2) % 4
    diag = (core + 2) % 4
    has_left, has_right = b > 0, b < blocks - 1
    left, right = jnp.maximum(b - 1, 0), jnp.minimum(b + 1, blocks - 1)

    tiles = units // tile
    split = (tiles + 1) // 2
    halves = ((0, split), (split, tiles))

    def lanes(hh):
        return pl.ds(halves[hh][0] * tile, (halves[hh][1] - halves[hh][0]) * tile)

    def w_copies(t, slot):
        where = pl.ds(t * tile, tile)
        return (
            pltpu.make_async_copy(gate_ref.at[where, :], w_gate.at[slot], w_sem.at[slot, 0]),
            pltpu.make_async_copy(up_ref.at[where, :], w_up.at[slot], w_sem.at[slot, 1]),
            pltpu.make_async_copy(down_ref.at[:, where], w_down.at[slot], w_sem.at[slot, 2]),
        )

    def remote(src, dst, send, recv, **to):
        return pltpu.make_async_remote_copy(
            src_ref=src, dst_ref=dst, send_sem=send, recv_sem=recv, device_id=to, device_id_type=MESH
        )

    def mine(j):
        return first_ref.at[:, pl.ds(j * rows, rows), :]

    def raw_local(j):
        return pltpu.make_async_copy(mine(j), raw.at[j, a], raw_here.at[j])

    def raw_to_chip(j):
        return remote(mine(j), raw.at[j, a], raw_send.at[j, 0], raw_recv.at[j, 0], aa=chip)

    def raw_to_core(j):
        return remote(mine(j), raw.at[j, a], raw_send.at[j, 1], raw_recv.at[j, 1], aa=core)

    def raw_on(j):
        return remote(raw.at[j, chip], raw.at[j, chip], raw_send.at[j, 2], raw_recv.at[j, 2], aa=core)

    def raw_start(j):
        if j < stages:
            raw_to_chip(j).start()
            raw_to_core(j).start()
            raw_local(j).start()

    def raw_forward(j):
        if j < stages:
            raw_to_chip(j).wait_recv()
            raw_on(j).start()

    def raw_finish(j):
        raw_local(j).wait()
        raw_to_core(j).wait_recv()
        raw_on(j).wait_recv()

    def permute(j):
        def step(n, _):
            at = n * e_tile
            total = jnp.zeros((3 * rows, e_tile), jnp.float32)
            for src in range(4):
                here = lax.broadcasted_iota(jnp.int32, (e_tile, columns), 0) + (a * columns + at)
                hit = here == perm_ref[src]
                onehot[src % 2] = jnp.where(hit, 1.0, 0.0).astype(jnp.bfloat16)
                total += lax.dot_general(
                    raw[j, src].reshape(3 * rows, columns), onehot[src % 2], NT_DIMS,
                    preferred_element_type=jnp.float32,
                )
            panel[j, :, pl.ds(b, 1), :, pl.ds(pl.multiple_of(at, e_tile), e_tile)] = (
                total.astype(jnp.bfloat16).reshape(3, 1, rows, e_tile)
            )
            return 0

        lax.fori_loop(0, columns // e_tile, step, 0)

    def z_copy(j, block, way, target):
        where = panel.at[j, :, block]
        return remote(where, where, z_send.at[j, way, block], z_recv.at[j, block], ba=target)

    def z_start(j):
        if j < stages:
            pl.when(has_right)(lambda: z_copy(j, b, 0, right).start())
            pl.when(has_left)(lambda: z_copy(j, b, 1, left).start())

    def hop(j, h):
        @pl.when(b - h >= 0)
        def _():
            block = jnp.maximum(b - h, 0)
            z_copy(j, block, 0, right).wait_recv()
            pl.when(has_right)(lambda: z_copy(j, block, 0, right).start())

        @pl.when(b + h < blocks)
        def _():
            block = jnp.minimum(b + h, blocks - 1)
            z_copy(j, block, 1, left).wait_recv()
            pl.when(has_left)(lambda: z_copy(j, block, 1, left).start())

    def hops(j, third):
        if j >= stages:
            return
        cuts = [1 + (blocks - 1) * i // 3 for i in range(4)]

        def step(h, _):
            hop(j, h)
            return 0

        lax.fori_loop(cuts[third], cuts[third + 1], step, 0)

    def z_done(j):
        def step(block, _):
            pl.when(jnp.logical_and(has_right, block <= b))(lambda: z_copy(j, block, 0, right).wait_send())
            pl.when(jnp.logical_and(has_left, block >= b))(lambda: z_copy(j, block, 1, left).wait_send())
            return 0

        lax.fori_loop(0, blocks, step, 0)

    def near_copies(j, hh):
        slot = j % 2
        return tuple(
            remote(
                part.at[slot, dest, :, :, lanes(hh)], near.at[slot, i, :, :, lanes(hh)],
                near_send.at[j, hh, i], near_recv.at[j, hh, i], aa=core,
            )
            for i, dest in enumerate((core, diag))
        )

    def far_copy(j, hh):
        return remote(
            part.at[j % 2, chip, :, :, lanes(hh)], far_ref.at[:, pl.ds(j * rows, rows), lanes(hh)],
            far_send.at[j, hh], far_recv.at[j, hh], aa=chip,
        )

    def own_copy(j, hh):
        return pltpu.make_async_copy(
            part.at[j % 2, a, :, :, lanes(hh)], own_ref.at[:, pl.ds(j * rows, rows), lanes(hh)], own_sem.at[j, hh]
        )

    def leave(j, hh):
        for copy in near_copies(j, hh):
            copy.wait_send()
        far_copy(j, hh).wait_send()
        own_copy(j, hh).wait()

    def product(j, hh):
        slot = j % 2
        if j >= 2:
            leave(j - 2, hh)

        def step(t, _):
            count = j * tiles + t
            now = count % 2

            @pl.when(count + 1 < stages * tiles)
            def _():
                for copy in w_copies((t + 1) % tiles, 1 - now):
                    copy.start()

            for copy in w_copies(t, now):
                copy.wait()
            lhs = [panel[j, kind].reshape(blocks * rows, columns) for kind in range(3)]
            total = lax.dot_general(lhs[0], w_gate[now], NT_DIMS, preferred_element_type=jnp.float32)
            total += lax.dot_general(lhs[1], w_up[now], NT_DIMS, preferred_element_type=jnp.float32)
            total += jnp.dot(lhs[2], w_down[now], preferred_element_type=jnp.float32)
            part[slot, :, :, :, pl.ds(pl.multiple_of(t * tile, tile), tile)] = total.reshape(4, group, rows, tile)
            return 0

        lax.fori_loop(*halves[hh], step, 0)
        if j >= 2:
            pl.semaphore_wait(credit.at[j - 2, hh], 1)
        for copy in near_copies(j, hh):
            copy.start()

    def combine(j, hh):
        slot = j % 2
        for copy in near_copies(j, hh):
            copy.wait_recv()

        def step(t, _):
            where = pl.ds(pl.multiple_of(t * tile, tile), tile)
            for i, dest in ((1, chip), (0, a)):
                part[slot, dest, :, :, where] = part[slot, dest, :, :, where] + near[slot, i, :, :, where]
            return 0

        lax.fori_loop(*halves[hh], step, 0)
        far_copy(j, hh).start()
        own_copy(j, hh).start()
        if j + 2 < stages:
            pl.semaphore_signal(credit.at[j, hh], inc=1, device_id={"aa": core}, device_id_type=MESH)

    for copy in w_copies(0, 0):
        copy.start()
    barrier = pltpu.get_barrier_semaphore()
    pl.semaphore_signal(barrier, inc=1, device_id={"aa": core}, device_id_type=MESH)
    pl.semaphore_signal(barrier, inc=1, device_id={"aa": chip}, device_id_type=MESH)
    pl.when(has_left)(
        lambda: pl.semaphore_signal(barrier, inc=1, device_id={"ba": left}, device_id_type=MESH)
    )
    pl.when(has_right)(
        lambda: pl.semaphore_signal(barrier, inc=1, device_id={"ba": right}, device_id_type=MESH)
    )
    pl.semaphore_wait(barrier, 2 + has_left.astype(jnp.int32) + has_right.astype(jnp.int32))

    raw_start(0)
    raw_start(1)
    raw_forward(0)
    raw_finish(0)
    raw_start(2)
    permute(0)
    z_start(0)
    raw_forward(1)
    for j in range(stages + 1):
        if j + 1 < stages:
            raw_finish(j + 1)
            raw_start(j + 3)
            permute(j + 1)
            raw_forward(j + 2)
        if j >= 2:
            combine(j - 2, 1)
        hops(j, 0)
        if j >= 1:
            product(j - 1, 0)
        hops(j, 1)
        z_start(j + 1)
        if j >= 1:
            product(j - 1, 1)
            combine(j - 1, 0)
        hops(j, 2)
    combine(stages - 1, 1)
    for j in range(max(stages - 2, 0), stages):
        leave(j, 0)
        leave(j, 1)
    for j in range(stages):
        raw_to_chip(j).wait_send()
        raw_to_core(j).wait_send()
        raw_on(j).wait_send()
        z_done(j)
        far_copy(j, 0).wait_recv()
        far_copy(j, 1).wait_recv()


def shards(mesh, gate_first, up_first, down_first, gate_second, up_second, down_second, perm):
    blocks = mesh.shape["ba"]
    assert mesh.shape["aa"] == 4 and blocks % 4 == 0
    rows_dev, columns = gate_first.shape
    units = gate_second.shape[0]
    stages = max(1, min(4, rows_dev // 16))
    rows = rows_dev // stages
    group = blocks // 4
    tile = next(t for t in (256, 128) if units % t == 0)
    e_tile = 256
    first = jnp.stack([gate_first, up_first, jnp.transpose(down_first)])
    order = perm.reshape(4, 1, columns)
    bf16, f32, dma = jnp.bfloat16, jnp.float32, pltpu.SemaphoreType.DMA
    anywhere = pl.BlockSpec(memory_space=pl.ANY)
    sums = jax.ShapeDtypeStruct((group, rows_dev, units), f32)
    own, far = pl.pallas_call(
        functools.partial(kernel, stages, blocks, rows, tile, e_tile),
        out_shape=[sums, sums],
        in_specs=[anywhere, pl.BlockSpec(memory_space=pltpu.VMEM), anywhere, anywhere, anywhere],
        out_specs=[anywhere, anywhere],
        scratch_shapes=[
            pltpu.VMEM((stages, 4, 3, rows, columns), bf16),
            pltpu.VMEM((stages, 3, blocks, rows, columns), bf16),
            pltpu.VMEM((2, 4, group, rows, units), f32),
            pltpu.VMEM((2, 2, group, rows, units), f32),
            pltpu.VMEM((2, tile, columns), bf16),
            pltpu.VMEM((2, tile, columns), bf16),
            pltpu.VMEM((2, columns, tile), bf16),
            pltpu.VMEM((2, e_tile, columns), bf16),
            dma((2, 3)),
            dma((stages,)),
            dma((stages, 3)),
            dma((stages, 3)),
            dma((stages, blocks)),
            dma((stages, 2, blocks)),
            dma((stages, 2, 2)),
            dma((stages, 2, 2)),
            dma((stages, 2)),
            dma((stages, 2)),
            dma((stages, 2)),
            pltpu.SemaphoreType.REGULAR((stages, 2)),
        ],
        compiler_params=pltpu.CompilerParams(
            collective_id=0, has_side_effects=True, vmem_limit_bytes=60 * 1024 * 1024
        ),
        cost_estimate=pl.CostEstimate(
            flops=6 * blocks * rows_dev * units * columns, bytes_accessed=6 * units * columns * stages, transcendentals=0
        ),
    )(first, order, gate_second, up_second, down_second)
    return (own + far).reshape(group * rows_dev, units)


def solution(mesh):
    placed = (
        P(("grp", "ba"), "aa"),
        P(("grp", "ba"), "aa"),
        P("aa", ("grp", "ba")),
        P(("grp", "ba"), "aa"),
        P(("grp", "ba"), "aa"),
        P("aa", ("grp", "ba")),
        P("grp"),
    )
    return jax.shard_map(
        functools.partial(shards, mesh), mesh=mesh, in_specs=placed, out_specs=P(("grp", "aa"), "ba"), check_vma=False
    )
```

time: 871 us -> 357 us (0.41)
  waiting for transfers between devices: 546 us -> 0 us
  Pallas kernels: 0 us -> 342 us
  local copies, waits for them, and re-layouts: 169 us -> 1.48 us
  matrix products: 124 us -> 0 us
  between operations: 13.2 us -> 0.02 us
    pallas_call x0 -> x1, Pallas kernels: none -> 342 us  [shards(): pl.pallas_call(functools.partial(kernel, stages, blocks, rows, tile, e_ti...]
    all_gather x2 -> x0, waiting for transfers between devices: 340 us -> none  [the longest x1 286 us: shards(): gathered = lax.all_gather(reordered, 'ba', axis=1, tiled=True)]
    reduce_scatter x1 -> x0, waiting for transfers between devices: 206 us -> none  [shards(): lax.psum_scatter(partial_cost(gathered, gate_second, up_second, down_seco...]
    dot_general x3 -> x0, matrix products: 124 us -> none  [the longest x1 51 us: partial_cost(): lax.dot_general(panel_rows[1], up_second, contract, preferred_element_typ...]
    slice x4 -> x0, local copies, waits for them, and re-layouts: 90.1 us -> none  [the longest x2 50.2 us: partial_cost(): panel_rows[1]]
    scatter x1 -> x0, local copies, waits for them, and re-layouts: 30.5 us -> none  [shards(): jnp.zeros((count_d,), jnp.int32).at[perm]]
    all_gather x1 -> x0, local copies, waits for them, and re-layouts: 24.9 us -> none  [shards(): features = lax.all_gather(stacked, 'aa', axis=2, tiled=True)]
    gather x1 -> x0, local copies, waits for them, and re-layouts: 22.3 us -> none  [shards(): reordered = jnp.take(features, chosen, axis=2)]
  transfers between devices with their start and end apart: 3 -> 0, of which waited for: 3 -> 0; matrix products, arithmetic and copies ran while one was open for 4% -> 0% of each run, Pallas kernels for 0% -> 0%
where the time goes in v1:
time: 357 us
  Pallas kernels  342 us (96%)
  other arithmetic  12.9 us (4%)
    pallas_call x1, Pallas kernels, shards(): pl.pallas_call(functools.partial(kernel, stages, blocks, rows, tile, e_ti...  342 us
    reshape x1, other arithmetic, shards(): return (own + far).reshape(group * rows_dev, units)  9.34 us

profile of v1, /device:TPU:1, one launch (start us, length us, event | category | flops | bytes accessed | tf_op | source)
XLA Modules:
  0.0 356.6 jit_solution(7159508963154874054)
XLA Ops:
  0.0 1.5 copy.8
  1.5 3.5 pad_maximum_fusion.first_ref
  5.0 342.2 %shard_map.73 = (f32[1,256,7168]{2,1,0:T(8,128)}, f32[1,256,7168]{2,1,0:T(8,128)}) custom-call(bf16[3,256,2048]{2,1,0:T(8,128)(2,1)} %pad_maximum_fusion.first_ref, s32[4,1,2048]{2,1,0:T(1,128)} %bitcast.11, bf16[7168,2048]{1,0:T(8,128)(2,1)} %gate_ref.1, bf16[7168,2048]{1,0:T(8,128)(2,1)} %up_ref.1, bf16[2048,7168]{1,0:T(8,128)(2,1)} %down_ref.1), custom_call_target="tpu_custom_call" | custom-call | flops 90194313216 | bytes 352321536 | tf_op jit(solution)/shard_map/pallas_call | solution.py:283
  347.3 9.3 %add_bitcast_fusion = f32[256,7168]{1,0:T(8,128)} fusion(f32[1,256,7168]{2,1,0:T(8,128)} %get-tuple-element.7, f32[1,256,7168]{2,1,0:T(8,128)} %get-tuple-element.8), kind=kLoop, calls=%fused_computation | loop fusion | flops 1835008 | bytes 22020096 | tf_op jit(solution)/shard_map/reshape | solution.py:317

commit v2 on v1

--- a/solution.py
+++ b/solution.py
@@ -54,16 +54,16 @@
         return first_ref.at[:, pl.ds(j * rows, rows), :]
 
     def raw_local(j):
-        return pltpu.make_async_copy(mine(j), raw.at[j, a], raw_here.at[j])
+        return pltpu.make_async_copy(mine(j), raw.at[a, j], raw_here.at[j])
 
     def raw_to_chip(j):
-        return remote(mine(j), raw.at[j, a], raw_send.at[j, 0], raw_recv.at[j, 0], aa=chip)
+        return remote(mine(j), raw.at[a, j], raw_send.at[j, 0], raw_recv.at[j, 0], aa=chip)
 
     def raw_to_core(j):
-        return remote(mine(j), raw.at[j, a], raw_send.at[j, 1], raw_recv.at[j, 1], aa=core)
+        return remote(mine(j), raw.at[a, j], raw_send.at[j, 1], raw_recv.at[j, 1], aa=core)
 
     def raw_on(j):
-        return remote(raw.at[j, chip], raw.at[j, chip], raw_send.at[j, 2], raw_recv.at[j, 2], aa=core)
+        return remote(raw.at[chip, j], raw.at[chip, j], raw_send.at[j, 2], raw_recv.at[j, 2], aa=core)
 
     def raw_start(j):
         if j < stages:
@@ -81,20 +81,20 @@
         raw_to_core(j).wait_recv()
         raw_on(j).wait_recv()
 
-    def permute(j):
+    def permute(j, count=1):
         def step(n, _):
             at = n * e_tile
-            total = jnp.zeros((3 * rows, e_tile), jnp.float32)
+            total = jnp.zeros((count * 3 * rows, e_tile), jnp.float32)
+            here = lax.broadcasted_iota(jnp.int32, (e_tile, columns), 0)
             for src in range(4):
-                here = lax.broadcasted_iota(jnp.int32, (e_tile, columns), 0) + (a * columns + at)
-                hit = here == perm_ref[src]
+                hit = here == perm_ref[src] - (a * columns + at)
                 onehot[src % 2] = jnp.where(hit, 1.0, 0.0).astype(jnp.bfloat16)
                 total += lax.dot_general(
-                    raw[j, src].reshape(3 * rows, columns), onehot[src % 2], NT_DIMS,
+                    raw[src, j : j + count].reshape(count * 3 * rows, columns), onehot[src % 2], NT_DIMS,
                     preferred_element_type=jnp.float32,
                 )
-            panel[j, :, pl.ds(b, 1), :, pl.ds(pl.multiple_of(at, e_tile), e_tile)] = (
-                total.astype(jnp.bfloat16).reshape(3, 1, rows, e_tile)
+            panel[j : j + count, :, pl.ds(b, 1), :, pl.ds(pl.multiple_of(at, e_tile), e_tile)] = (
+                total.astype(jnp.bfloat16).reshape(count, 3, 1, rows, e_tile)
             )
             return 0
 
@@ -236,11 +236,12 @@
     z_start(0)
     raw_forward(1)
     for j in range(stages + 1):
-        if j + 1 < stages:
-            raw_finish(j + 1)
-            raw_start(j + 3)
-            permute(j + 1)
-            raw_forward(j + 2)
+        if j == 0 and stages > 1:
+            raw_finish(1)
+            for later in range(3, stages):
+                raw_start(later)
+            permute(1)
+            raw_forward(2)
         if j >= 2:
             combine(j - 2, 1)
         hops(j, 0)
@@ -248,6 +249,12 @@
             product(j - 1, 0)
         hops(j, 1)
         z_start(j + 1)
+        if j == 0 and stages > 2:
+            for later in range(2, stages):
+                if later > 2:
+                    raw_forward(later)
+                raw_finish(later)
+            permute(2, stages - 2)
         if j >= 1:
             product(j - 1, 1)
             combine(j - 1, 0)
@@ -286,7 +293,7 @@
         in_specs=[anywhere, pl.BlockSpec(memory_space=pltpu.VMEM), anywhere, anywhere, anywhere],
         out_specs=[anywhere, anywhere],
         scratch_shapes=[
-            pltpu.VMEM((stages, 4, 3, rows, columns), bf16),
+            pltpu.VMEM((4, stages, 3, rows, columns), bf16),
             pltpu.VMEM((stages, 3, blocks, rows, columns), bf16),
             pltpu.VMEM((2, 4, group, rows, units), f32),
             pltpu.VMEM((2, 2, group, rows, units), f32),

time: 357 us -> 356 us (level)
  no operation moved by 1% of the time
where the time goes in v2:
time: 356 us; the launch traced here: 355 us
  Pallas kernels  341 us (96%)
  other arithmetic  12.9 us (4%)
    pallas_call x1, Pallas kernels, shards(): pl.pallas_call(functools.partial(kernel, stages, blocks, rows, tile, e_ti...  341 us
    reshape x1, other arithmetic, shards(): return (own + far).reshape(group * rows_dev, units)  9.34 us

profile of v2, /device:TPU:1, one launch (start us, length us, event | category | flops | bytes accessed | tf_op | source)
XLA Modules:
  0.0 355.3 jit_solution(14350950820420086447)
XLA Ops:
  0.0 1.5 copy.8
  1.5 3.5 pad_maximum_fusion.first_ref
  5.0 340.9 %shard_map.73 = (f32[1,256,7168]{2,1,0:T(8,128)}, f32[1,256,7168]{2,1,0:T(8,128)}) custom-call(bf16[3,256,2048]{2,1,0:T(8,128)(2,1)} %pad_maximum_fusion.first_ref, s32[4,1,2048]{2,1,0:T(1,128)} %bitcast.11, bf16[7168,2048]{1,0:T(8,128)(2,1)} %gate_ref.1, bf16[7168,2048]{1,0:T(8,128)(2,1)} %up_ref.1, bf16[2048,7168]{1,0:T(8,128)(2,1)} %down_ref.1), custom_call_target="tpu_custom_call" | custom-call | flops 90194313216 | bytes 352321536 | tf_op jit(solution)/shard_map/pallas_call | solution.py:290
  346.0 9.3 %add_bitcast_fusion = f32[256,7168]{1,0:T(8,128)} fusion(f32[1,256,7168]{2,1,0:T(8,128)} %get-tuple-element.7, f32[1,256,7168]{2,1,0:T(8,128)} %get-tuple-element.8), kind=kLoop, calls=%fused_computation | loop fusion | flops 1835008 | bytes 22020096 | tf_op jit(solution)/shard_map/reshape | solution.py:324
